TPU v7x, 32 devices: a whole 2x2x4 slice. The times are simulated.
32 devices in a mesh: cfg: 2 (over y), slab: 4 (over z), tile: 2 (over x), spin: 2 (over core).
Axes of the slice: x: 2, y: 2, z: 4, core: 2. Of those that a mesh axis runs over, the one named last changes fastest.
Arguments:
- eigenvectors: bfloat16 [4, 2, 3, 8, 1024, 256], P(('cfg', 'tile'), None, None, 'slab', 'spin'), parts along dimension 0, may hold values from -6 to 6
- gauge_links: float32 [4, 2, 3, 3, 8, 1024], P(('cfg', 'tile'), None, None, None, 'slab', 'spin'), parts along dimension 0, may hold values from -2.5 to 2.5
- momenta: int32 [2, 3], replicated, may hold values from -2 to 2
- displacement: int32 [2], replicated, may hold values from 1 to 2, as said below
- slice_pairs: int32 [4, 2], P('tile'), may hold values from 0 to 1, as said below
- perambulators: bfloat16 [8, 2, 1024, 1024], P(('cfg', 'tile'), None, 'spin', 'slab'), parts along dimension 0, may hold values from -6 to 6
Outputs:
- meson_blocks: bfloat16 [8, 2, 1024, 1024], P(('cfg', 'tile'), None, 'spin', 'slab'), parts along dimension 0
There are 2 independent parts, one for each index of `cfg`. A program takes and returns all parts, laid end to end along the dimension named above; an argument that names none is the same for every part. Nothing has to cross between parts.
Inputs may be any that keep to these rules, and one draw needn't show every extreme that they name: `displacement`: the entries are 1 and 2 in some order, so one elemental is displaced forward and the other backward. `slice_pairs`: column 0 is the sink slice and column 1 the source slice; every pair of slices in 0 to 1 appears exactly once.
All inputs are finite; a program needn't handle non-finite values.
Results may differ from a plain program's by a relative error of at most 0.008.
Values may be sent and summed in bfloat16 or wider, within the bound.
A program may use at most 64 MiB of HBM per device.

v0:
```python
import math

import jax
import jax.numpy as jnp
from jax import lax
from jax.sharding import PartitionSpec as P

NS = 4
LY = 32
LZ = 32


def from_behind(x, axis, by):
    count = lax.axis_size(axis)
    return lax.ppermute(x, axis, [(i, (i + by) % count) for i in range(count)])


def color_apply(link_field, vectors_here, adjoint):
    field_real = vectors_here[0].astype(jnp.float32)
    field_imag = vectors_here[1].astype(jnp.float32)
    if adjoint:
        link_real = jnp.swapaxes(link_field[0], 0, 1)
        link_imag = -jnp.swapaxes(link_field[1], 0, 1)
    else:
        link_real = link_field[0]
        link_imag = link_field[1]
    out_real = jnp.zeros(field_real.shape, jnp.float32)
    out_imag = jnp.zeros(field_real.shape, jnp.float32)
    for color_in in range(3):
        column_real = link_real[:, color_in][:, :, :, None]
        column_imag = link_imag[:, color_in][:, :, :, None]
        out_real = (
            out_real + column_real * field_real[color_in] - column_imag * field_imag[color_in]
        )
        out_imag = (
            out_imag + column_real * field_imag[color_in] + column_imag * field_real[color_in]
        )
    return jnp.stack([out_real, out_imag])


def phase_table(momenta, x_global, yz_global, extent_x, extent_y, extent_z):
    y_coord = yz_global // extent_z
    z_coord = yz_global % extent_z
    wave_x = jnp.mod(momenta[:, 0:1] * x_global[None, :], extent_x)
    wave_y = jnp.mod(momenta[:, 1:2] * y_coord[None, :], extent_y)
    wave_z = jnp.mod(momenta[:, 2:3] * z_coord[None, :], extent_z)
    numerator = (
        wave_x[:, :, None] * (extent_y * extent_z)
        + (wave_y * (extent_x * extent_z) + wave_z * (extent_x * extent_y))[:, None, :]
    )
    angle = numerator.astype(jnp.float32) * (2.0 * math.pi / (extent_x * extent_y * extent_z))
    return (jnp.cos(angle), -jnp.sin(angle))


def elemental_reindexed(
    vectors_here, shifted_up, forward, back_local, rot_here, rot_next, displacement
):
    vector_count = vectors_here.shape[-1]
    numbers = (((0,), (0,)), ((), ()))
    backward_here = back_local.astype(jnp.float32)
    results = []
    for which in range(displacement.shape[0]):
        is_forward = displacement[which] == 1
        row_field = jnp.where(is_forward, vectors_here, shifted_up)
        moved = jnp.where(is_forward, forward, backward_here)
        cosine = jnp.where(is_forward, rot_here[0][which], rot_next[0][which])[None, :, :, None]
        sine = jnp.where(is_forward, rot_here[1][which], rot_next[1][which])[None, :, :, None]
        phased_real = (
            (cosine * moved[0] - sine * moved[1]).astype(jnp.bfloat16).reshape(-1, vector_count)
        )
        phased_imag = (
            (cosine * moved[1] + sine * moved[0]).astype(jnp.bfloat16).reshape(-1, vector_count)
        )
        field_real = row_field[0].reshape(-1, vector_count)
        field_imag = row_field[1].reshape(-1, vector_count)
        top_block = jnp.concatenate([phased_real, phased_imag], axis=1)
        bottom_block = jnp.concatenate([phased_imag, -phased_real], axis=1)
        first = lax.dot_general(field_real, top_block, numbers, preferred_element_type=jnp.float32)
        second = lax.dot_general(
            field_imag, bottom_block, numbers, preferred_element_type=jnp.float32
        )
        results.append(first + second)
    return jnp.concatenate(results, axis=1)


def complex_product(form, first_real, first_imag, second_real, second_imag):
    out_real = jnp.einsum(
        form, first_real, second_real, preferred_element_type=jnp.float32
    ) - jnp.einsum(form, first_imag, second_imag, preferred_element_type=jnp.float32)
    out_imag = jnp.einsum(
        form, first_real, second_imag, preferred_element_type=jnp.float32
    ) + jnp.einsum(form, first_imag, second_real, preferred_element_type=jnp.float32)
    return (out_real, out_imag)


def body(eigenvectors, gauge_links, momenta, displacement, slice_pairs, perambulators):
    vectors_here = eigenvectors[0]
    link_field = gauge_links[0]
    planes = vectors_here.shape[2]
    sites_dev = vectors_here.shape[3]
    vectors = vectors_here.shape[4]
    slab_count = lax.axis_size("slab")
    lattice_x = planes * slab_count
    normalize = 1.0 / math.sqrt(3072 * lattice_x * LY * LZ)
    next_rim = from_behind(vectors_here[:, :, 0:1], "slab", -1)
    shifted_up = jnp.concatenate([vectors_here[:, :, 1:], next_rim], axis=2)
    forward = color_apply(link_field, shifted_up, False)
    back_local = lax.optimization_barrier(
        color_apply(link_field, vectors_here, True).astype(jnp.bfloat16)
    )
    x_global = lax.axis_index("slab") * planes + jnp.arange(planes, dtype=jnp.int32)
    yz_global = lax.axis_index("spin") * sites_dev + jnp.arange(sites_dev, dtype=jnp.int32)
    rot_real, rot_imag = phase_table(momenta, x_global, yz_global, lattice_x, LY, LZ)
    next_real, next_imag = phase_table(momenta, x_global + 1, yz_global, lattice_x, LY, LZ)
    partial_sum = (
        elemental_reindexed(
            vectors_here,
            shifted_up,
            forward,
            back_local,
            (rot_real, rot_imag),
            (next_real, next_imag),
            displacement,
        )
        * normalize
    )
    slices = lax.axis_size("tile")
    summed = lax.psum(partial_sum, ("slab", "spin"))
    elemental_table = lax.all_gather(summed.astype(jnp.bfloat16)[None], "tile", axis=0, tiled=True)
    pair_count = perambulators.shape[0]
    spin_rows = perambulators.shape[2] // vectors
    columns = perambulators.shape[3]
    slice_ids = jnp.arange(slices, dtype=jnp.int32)[None, :]
    onehot_sink = (slice_pairs[:, 0:1] == slice_ids).astype(jnp.bfloat16)
    onehot_source = (slice_pairs[:, 1:2] == slice_ids).astype(jnp.bfloat16)
    chosen_sink = jnp.einsum(
        "pt,tvc->pvc",
        onehot_sink,
        elemental_table[:, :, : 2 * vectors],
        preferred_element_type=jnp.float32,
    ).astype(jnp.bfloat16)
    chosen_source = jnp.einsum(
        "pt,tvc->pvc",
        onehot_source,
        elemental_table[:, :, 2 * vectors :],
        preferred_element_type=jnp.float32,
    ).astype(jnp.bfloat16)
    sink_real = chosen_sink[:, :, :vectors]
    sink_imag = chosen_sink[:, :, vectors:]
    source_real = chosen_source[:, :, :vectors]
    source_imag = chosen_source[:, :, vectors:]
    tau_real = perambulators[:, 0].reshape(pair_count, spin_rows, vectors, columns)
    tau_imag = perambulators[:, 1].reshape(pair_count, spin_rows, vectors, columns)
    left_real, left_imag = complex_product(
        "pvu,psuc->psvc", sink_real, sink_imag, tau_real, tau_imag
    )
    left_block = (
        jnp.stack([left_real, left_imag], axis=1)
        .reshape(pair_count, 2, spin_rows * vectors, columns)
        .astype(jnp.bfloat16)
    )
    per_vector = columns // NS
    first_vector = lax.axis_index("slab") * per_vector
    block_real = lax.dynamic_slice_in_dim(source_real, first_vector, per_vector, 2)
    block_imag = lax.dynamic_slice_in_dim(source_imag, first_vector, per_vector, 2)
    left_split = left_block.reshape(pair_count, 2, spin_rows * vectors, per_vector, NS)
    piece = lax.all_gather(left_split, "slab", axis=3, tiled=True)
    term_real, term_imag = complex_product(
        "prvb,pvw->prwb", piece[:, 0], piece[:, 1], block_real, block_imag
    )
    meson_blocks = (
        jnp.stack([term_real, term_imag], axis=1)
        .reshape(pair_count, 2, spin_rows * vectors, columns)
        .astype(jnp.bfloat16)
    )
    return meson_blocks


def solution(mesh):
    return jax.shard_map(
        body,
        mesh=mesh,
        in_specs=(
            P(("cfg", "tile"), None, None, "slab", "spin", None),
            P(("cfg", "tile"), None, None, None, "slab", "spin"),
            P(),
            P(),
            P("tile", None),
            P(("cfg", "tile"), None, "spin", "slab"),
        ),
        out_specs=P(("cfg", "tile"), None, "spin", "slab"),
        check_vma=False,
    )
```

profile of v0, /device:TPU:0, one launch (start us, length us, event | category | flops | bytes accessed | tf_op | source)
XLA Modules:
  0.0 280.4 jit_solution(5339265094451365318)
XLA Ops:
  6.5 3.9 %fusion.106 = (bf16[2,3,1,512,256]{4,3,2,1,0:T(8,128)(2,1)}, bf16[2,3,1,512,256]{4,3,2,1,0:T(8,128)(2,1)}) fusion(bf16[2,3,2,512,256]{4,3,2,1,0:T(8,128)(2,1)} %bitcast.197), kind=kLoop, calls=%fused_computation.196 | loop fusion | bytes 6291456 | tf_op jit(solution)/shard_map/slice | solution.py:106
  10.4 5.0 %collective-permute-start = (bf16[2,3,1,512,256]{4,3,2,1,0:T(8,128)(2,1)}, bf16[2,3,1,512,256]{4,3,2,1,0:T(8,128)(2,1)}, u32[]{:S(2)}, u32[]{:S(2)}) collective-permute-start(bf16[2,3,1,512,256]{4,3,2,1,0:T(8,128)(2,1)} %get-tuple-element.49), channel_id=1, source_target_pairs={{0,12},{4,0},{8,4},{12,8},{1,13},{5,1},{9,5},{13,9},{2,14},{6,2},{... | collective-permute-start | bytes 4718600 | tf_op jit(solution)/shard_map/ppermute | solution.py:15
  15.5 3.3 %slice_convert_fusion.1 = (f32[1,1,3,2,512,256]{5,4,3,2,1,0:T(8,128)}, f32[1,1,3,2,512,256]{5,4,3,2,1,0:T(8,128)}) fusion(bf16[1,2,3,2,512,256]{5,4,3,2,1,0:T(8,128)(2,1)S(1)} %copy-done), kind=kLoop, calls=%fused_computation.60 | loop fusion | flops 1572864 | bytes 9437184 | tf_op jit(solution)/shard_map/convert_element_type | solution.py:19
  18.9 3.6 %slice_bitcast_fusion.4 = (f32[2,512,256]{2,1,0:T(8,128)S(1)}, f32[2,512,256]{2,1,0:T(8,128)S(1)}, f32[2,512,256]{2,1,0:T(8,128)S(1)}, f32[2,512,256]{2,1,0:T(8,...) fusion(f32[1,1,3,2,512,256]{5,4,3,2,1,0:T(8,128)} %get-tuple-element.47, ...), kind=kLoop, calls=%fused_computation.81 | loop fusion | bytes 12582912 | tf_op jit(solution)/shard_map/mul | solution.py:33
  22.5 3.2 %subtract_convert_fusion = (bf16[1,3,2,512,256]{4,3,2,1,0:T(8,128)(2,1)S(1)}, bf16[1,3,2,512,256]{4,3,2,1,0:T(8,128)(2,1)S(1)}) fusion(f32[2,512,256]{2,1,0:T(8,128)S(1)} %get-tuple-element.44, f32[3,2,512]{2,1,0:T(2,128)S(1)} %get-tuple-element.71, f32[2,512,256]{2,1,0:T(8,128)S(1)} %get-tuple-element.92, f32[3,2,512]{2,1,0:T(2,128)S(1)} %get-tuple-element.98, ...), kind=kLoop, calls=%fused_computation.42 | loop fusion | flops 18874368 | bytes 9510912 | tf_op jit(solution)/shard_map/convert.12
  25.7 2.0 pad_maximum_fusion.2
  27.7 0.6 fusion.110
  30.5 19.0 %collective-permute-done = bf16[2,3,1,512,256]{4,3,2,1,0:T(8,128)(2,1)} collective-permute-done((bf16[2,3,1,512,256]{4,3,2,1,0:T(8,128)(2,1)}, bf16[2,3,1,512,256]{4,3,2,1,0:T(8,128)(2,1)}, u32[]{:S(2)}, u32[]{:S(2)}) %collective-permute-start) | collective-permute-done | bytes 1572896 | tf_op jit(solution)/shard_map/ppermute | solution.py:15
  49.5 1.8 fusion.33
  51.2 0.4 slice_bitcast_fusion.10
  51.7 5.6 %multiply_subtract_fusion = (f32[1,3,2,512,256]{4,3,2,1,0:T(8,128)}, f32[1,3,2,512,256]{4,3,2,1,0:T(8,128)}) fusion(f32[2,512,256]{2,1,0:T(8,128)S(1)} %get-tuple-element.36, f32[3,2,512]{2,1,0:T(2,128)S(1)} %get-tuple-element.65, f32[2,512,256]{2,1,0:T(8,128)S(1)} %get-tuple-element.101, f32[3,2,512]{2,1,0:T(2,128)S(1)} %get-tuple-element.95, ...), kind=kLoop, calls=%fused_computation.44 | loop fusion | flops 17301504 | bytes 12656640 | tf_op jit(solution)/shard_map/sub | solution.py:33
  57.2 7.8 %convert_select_fusion.1 = (f32[2,3,2,512,256]{4,3,2,1,0:T(8,128)}, f32[2,3,2,512,256]{4,3,2,1,0:T(8,128)S(1)}) fusion(bf16[2,3,2,512,256]{4,3,2,1,0:T(8,128)(2,1)} %pad_maximum_fusion.2, f32[1,3,2,512,256]{4,3,2,1,0:T(8,128)} %get-tuple-element.17, f32[1,3,2,512,256]{4,3,2,1,0:T(8,128)} %get-tuple-element.16, pred[]{:T(512)} %bitcast.1, pred[]{:T(512)} %bitcast.38), kind=kLoop, calls=%fused_computation.1 | loop fusion | flops 6291456 | bytes 22020098 | tf_op jit(solution)/shard_map/jit(_where)/select_n | solution.py:65
  65.0 3.6 %fusion.101 = (f32[1,3,2,512,256]{4,3,2,1,0:T(8,128)S(1)}, f32[1,3,2,512,256]{4,3,2,1,0:T(8,128)S(1)}) fusion(f32[2,3,2,512,256]{4,3,2,1,0:T(8,128)} %get-tuple-element.14), kind=kLoop, calls=%fused_computation.191 | loop fusion | bytes 12582912 | tf_op jit(solution)/shard_map/slice | solution.py:69
  68.7 1.6 fusion.23
  70.3 1.6 fusion.97
  72.0 0.8 fusion.102
  72.8 1.6 fusion.19
  74.4 1.6 fusion.99
  76.0 1.6 broadcast_select_fusion.1
  77.7 0.5 fusion.104
  78.2 1.0 fusion.4
  79.2 1.0 fusion.61
  80.2 1.0 fusion.12
  81.2 1.0 fusion.58
  82.4 60.3 %all-reduce.1 = bf16[256,1024]{1,0:T(8,128)(2,1)} all-reduce(f32[256,1024]{1,0:T(8,128)S(1)} %maximum_multiply_fusion), channel_id=1, replica_groups=mesh['cfg'=2,'slab'=4,'tile'=2,'spin'=2] {'slab','spin'}, use_global_device_ids=true, to_apply=%region_0.1 | all-reduce | flops 262144 | bytes 1572864 | tf_op jit(solution)/shard_map/psum | solution.py:128
  143.0 20.3 %all-gather.6.cloned.1.call-done = bf16[512,1024]{1,0:T(8,128)(2,1)} async-done(((bf16[256,1024]{1,0:T(8,128)(2,1)}), bf16[512,1024]{1,0:T(8,128)(2,1)}) %all-gather.6.cloned.1.call-update) | async-done | bytes 1048592 | tf_op jit(solution)/shard_map/all_gather | solution.py:129
  163.3 2.1 fusion.108
  165.3 0.8 convolution_convert_fusion
  166.1 0.4 slice_bitcast_fusion.12
  167.1 1.1 fusion.51
  168.2 1.3 copy.40
  170.2 0.4 copy.43
  171.0 0.7 pad_maximum_fusion.3
  171.7 1.6 copy.44
  173.3 0.8 convolution_convert_fusion.1
  174.1 0.4 fusion.109
  175.1 79.2 %all-gather.4.cloned.1.call-done = bf16[2,2,512,256,4]{2,4,1,0,3:T(4,128)(2,1)} async-done(((bf16[2,2,512,64,4]{2,4,1,0,3:T(4,128)(2,1)}), bf16[2,2,512,256,4]{2,4,1,0,3:T(4,128)(2,1)}) %all-gather.4.cloned.1.call-update) | async-done | bytes 4194320 | tf_op jit(solution)/shard_map/all_gather | solution.py:167
  254.3 4.0 %fusion.103 = (bf16[2,1,512,256,4]{2,4,1,0,3:T(4,128)(2,1)}, bf16[2,1,512,256,4]{2,4,1,0,3:T(4,128)(2,1)S(1)}) fusion(bf16[2,2,512,256,4]{2,4,1,0,3:T(4,128)(2,1)} %all-gather.4.cloned.1.call-done), kind=kLoop, calls=%fused_computation.193 | loop fusion | bytes 8388608 | tf_op jit(solution)/shard_map/slice | solution.py:169
  258.3 2.8 copy.81
  261.0 3.0 %copy.80 = bf16[2,1,512,256,4]{3,2,4,0,1:T(8,128)(2,1)S(1)} copy(bf16[2,1,512,256,4]{2,4,1,0,3:T(4,128)(2,1)} %get-tuple-element.26) | data formatting | bytes 4194304
  264.0 2.5 fusion.26
  266.5 0.8 fusion.24
  267.3 0.8 fusion.52
  268.1 0.5 copy.49
  268.6 0.8 fusion.55
  269.4 0.5 copy.52
  269.9 1.5 pad_maximum_fusion.4
  271.4 2.2 copy.53
  (55 shorter events, 3.5 us)
Async XLA Ops:
  6.5 156.7 %all-gather.6.cloned.1.call-start = ((), (), s32[]{:S(2)}) async-start(), calls=%async_computation.1 | async-start | bytes 1572864 | tf_op jit(solution)/shard_map/all_gather | solution.py:129
  6.5 9.0 %copy-start = (bf16[1,2,3,2,512,256]{5,4,3,2,1,0:T(8,128)(2,1)S(1)}, bf16[1,2,3,2,512,256]{5,4,3,2,1,0:T(8,128)(2,1)}, u32[]{:S(2)}) copy-start(bf16[1,2,3,2,512,256]{5,4,3,2,1,0:T(8,128)(2,1)} %param.6) | copy-start | bytes 9437188
  10.4 8.3 %copy-start.5 = (f32[1,2,3,3,2,512]{5,4,3,2,1,0:T(2,128)S(1)}, f32[1,2,3,3,2,512]{5,4,3,2,1,0:T(2,128)}, u32[]{:S(2)}) copy-start(f32[1,2,3,3,2,512]{5,4,3,2,1,0:T(2,128)} %param.7) | copy-start | bytes 221188
  10.4 39.0 %collective-permute-start = (bf16[2,3,1,512,256]{4,3,2,1,0:T(8,128)(2,1)}, bf16[2,3,1,512,256]{4,3,2,1,0:T(8,128)(2,1)}, u32[]{:S(2)}, u32[]{:S(2)}) collective-permute-start(bf16[2,3,1,512,256]{4,3,2,1,0:T(8,128)(2,1)} %get-tuple-element.49), channel_id=1, source_target_pairs={{0,12},{4,0},{8,4},{12,8},{1,13},{5,1},{9,5},{13,9},{2,14},{6,2},{... | collective-permute-start | bytes 4718600 | tf_op jit(solution)/shard_map/ppermute | solution.py:15
  25.7 2.0 copy-start.8
  25.7 3.9 %copy-start.6 = (s32[2,3]{1,0:T(2,128)S(1)}, s32[2,3]{1,0:T(2,128)}, u32[]{:S(2)}) copy-start(s32[2,3]{1,0:T(2,128)} %param.8) | copy-start | bytes 76
  25.7 23.8 %copy-start.2 = (bf16[2,3,1,512,256]{4,3,2,1,0:T(8,128)(2,1)S(1)}, bf16[2,3,1,512,256]{4,3,2,1,0:T(8,128)(2,1)}, u32[]{:S(2)}) copy-start(bf16[2,3,1,512,256]{4,3,2,1,0:T(8,128)(2,1)} %get-tuple-element.48) | copy-start | bytes 4718596
  82.2 60.5 %copy-start.7 = (s32[2,2]{1,0:T(2,128)S(1)}, s32[2,2]{1,0:T(2,128)}, u32[]{:S(2)}) copy-start(s32[2,2]{1,0:T(2,128)} %param.10) | copy-start | bytes 52
  82.2 60.7 %copy-start.3 = (bf16[2,2,512,256]{3,2,1,0:T(8,128)(2,1)S(1)}, bf16[2,2,512,256]{3,2,1,0:T(8,128)(2,1)}, u32[]{:S(2)}) copy-start(bf16[2,2,512,256]{3,2,1,0:T(8,128)(2,1)} %param.11) | copy-start | bytes 3145732
  142.6 111.6 %all-gather.4.cloned.1.call-start = ((), (), s32[]{:S(2)}) async-start(), calls=%async_computation | async-start | bytes 5242880 | tf_op jit(solution)/shard_map/all_gather | solution.py:167
  170.6 2.7 copy-start.4
  264.0 2.5 copy-start.1
Sparse Core Ops, SparseCore 0:
  142.8 20.4 all-gather.5
  173.4 80.7 all-gather.3
where the time goes:
time: 281 us; the launch traced here: 280 us
  waiting for transfers between devices  119 us (42%)
  blocking collectives  60.3 us (21%)
  other arithmetic  34.6 us (12%)
  local copies, waits for them, and re-layouts  34.5 us (12%)
  between operations  15.2 us (5%)
  matrix products  12.3 us (4%)
  starting transfers between devices  5.09 us (2%)
    all_gather x1, waiting for transfers between devices, body(): piece = lax.all_gather(left_split, 'slab', axis=3, tiled=True)  79.2 us
    psum x1, blocking collectives, body(): summed = lax.psum(partial_sum, ('slab', 'spin'))  60.3 us
    all_gather x1, waiting for transfers between devices, body(): lax.all_gather(summed.astype(jnp.bfloat16)[None], 'tile', axis=0, tiled=T...  20.3 us
    ppermute x1, waiting for transfers between devices, from_behind(): return lax.ppermute(x, axis, [(i, (i + by) % count) for i in range(count)])  19 us
    select_n x1, other arithmetic, elemental_reindexed(): moved = jnp.where(is_forward, forward, backward_here)  7.8 us
    unnamed x28, local copies, waits for them, and re-layouts  5.85 us
  transfers between devices with their start and end apart: 3, of which 3 were waited for; matrix products, arithmetic and copies ran while one was open for 6% of the time, Pallas kernels for 0%

commit v1 on v0

v1 whole, which is shorter than its diff:
```python
import functools
import math

import jax
import jax.numpy as jnp
from jax import lax
from jax.experimental import pallas as pl
from jax.experimental.pallas import tpu as pltpu
from jax.sharding import PartitionSpec as P

NS = 4
LY = 32
LZ = 32
MESH = pl.DeviceIdType.MESH
F32 = jnp.float32
BF16 = jnp.bfloat16
SITES = 16


def phase_table(momenta, x_global, yz_global, extent_x, extent_y, extent_z):
    y_coord = yz_global // extent_z
    z_coord = yz_global % extent_z
    wave_x = jnp.mod(momenta[:, 0:1] * x_global, extent_x)
    wave_y = jnp.mod(momenta[:, 1:2] * y_coord[None, :], extent_y)
    wave_z = jnp.mod(momenta[:, 2:3] * z_coord[None, :], extent_z)
    numerator = (
        wave_x[:, :, None] * (extent_y * extent_z)
        + (wave_y * (extent_x * extent_z) + wave_z * (extent_x * extent_y))[:, None, :]
    )
    angle = numerator.astype(F32) * (2.0 * math.pi / (extent_x * extent_y * extent_z))
    return (jnp.cos(angle), -jnp.sin(angle))


def remote(src, dst, send, recv, device):
    return pltpu.make_async_remote_copy(
        src_ref=src,
        dst_ref=dst,
        send_sem=send,
        recv_sem=recv,
        device_id=device,
        device_id_type=MESH,
    )


def dot(a, b, dims=((1,), (0,))):
    return lax.dot_general(a, b, (dims, ((), ())), preferred_element_type=F32)


def kernel(
    n, tiles, cores, normalize,
    v_ref, w_ref, p_ref, pairs_ref, disp_ref, out_ref,
    halo, ccat, wt, acc, parts, core_send, core_recv, total, rs_recv, table, pg, kbuf, rbuf,
    halo_sem, p_send, p_recv, core_sem, rs_send, rs_recv_sem, ag_send, ag_recv, bc_send, bc_recv,
):
    slab = lax.axis_index("slab")
    tile = lax.axis_index("tile")
    core = lax.axis_index("spin")
    _, _, planes, sites, nv = v_ref.shape
    pair_count, _, rows, cols = p_ref.shape
    quarter = nv // n
    others = [(dt, dc) for dt in range(tiles) for dc in range(cores) if (dt, dc) != (0, 0)]

    def along(d):
        return {"slab": lax.rem(slab + d, n)}

    def across(dt, dc):
        return {"tile": lax.rem(tile + dt, tiles), "spin": lax.rem(core + dc, cores)}

    barrier = pltpu.get_barrier_semaphore()
    for d in range(1, n):
        pl.semaphore_signal(barrier, inc=1, device_id=along(d), device_id_type=MESH)
    for dt, dc in others:
        pl.semaphore_signal(barrier, inc=1, device_id=across(dt, dc), device_id_type=MESH)
    pl.semaphore_wait(barrier, n - 1 + len(others))

    halo_copy = remote(
        v_ref.at[:, :, 0], halo, halo_sem.at[0], halo_sem.at[1], along(n - 1)
    )
    halo_copy.start()

    for plane in range(planes):
        wt[plane] = w_ref[plane].T

    for plane in range(planes):

        @pl.loop(0, sites // SITES)
        def _(i):
            here = pl.ds(pl.multiple_of(i * SITES, SITES), SITES)
            field = [
                [v_ref[part, c, plane, here, :].astype(F32) for part in range(2)]
                for c in range(3)
            ]
            weights = wt[plane, here, :]
            for e in range(2):
                for c_out in range(3):
                    real = None
                    imag = None
                    for c in range(3):
                        at = ((e * 3 + c_out) * 3 + c) * 2
                        w_real = weights[:, at : at + 1]
                        w_imag = weights[:, at + 1 : at + 2]
                        r = w_real * field[c][0] - w_imag * field[c][1]
                        m = w_real * field[c][1] + w_imag * field[c][0]
                        real = r if real is None else real + r
                        imag = m if imag is None else imag + m
                    ccat[plane * 3 + c_out, here, 2 * e * nv : (2 * e + 1) * nv] = real.astype(BF16)
                    ccat[plane * 3 + c_out, here, (2 * e + 1) * nv : (2 * e + 2) * nv] = imag.astype(BF16)

    acc[...] = jnp.zeros_like(acc)
    for plane in range(planes - 1):

        @pl.loop(0, 3)
        def _(c):
            for part in range(2):
                acc[part] += dot(
                    v_ref[part, c, plane + 1], ccat[plane * 3 + c], ((0,), (0,))
                )

    halo_copy.wait_send()
    p_copies = []
    for d in range(1, n):
        copy = remote(p_ref, pg.at[d - 1], p_send.at[d - 1], p_recv.at[d - 1], along(d))
        copy.start()
        p_copies.append(copy)
    halo_copy.wait_recv()

    @pl.loop(0, 3)
    def _(c):
        for part in range(2):
            acc[part] += dot(halo[part, c], ccat[(planes - 1) * 3 + c], ((0,), (0,)))

    for e in range(2):
        re_at = slice(2 * e * nv, (2 * e + 1) * nv)
        im_at = slice((2 * e + 1) * nv, (2 * e + 2) * nv)
        real = (acc[0, :, re_at] + acc[1, :, im_at]) * normalize
        imag = (acc[1, :, re_at] - acc[0, :, im_at]) * normalize
        forward = jnp.full((nv, nv), disp_ref[e], jnp.int32) == 1
        if e == 0:
            parts[0, e] = jnp.where(forward, real.T, real)
            parts[1, e] = jnp.where(forward, imag.T, -imag)
        else:
            parts[0, e] = jnp.where(forward, real, real.T)
            parts[1, e] = jnp.where(forward, imag, -imag.T)

    core_send[...] = parts[1 - core].astype(BF16)
    core_copy = remote(
        core_send, core_recv, core_sem.at[0], core_sem.at[1], {"spin": 1 - core}
    )
    core_copy.start()
    core_copy.wait_recv()
    total[...] = (parts[core] + core_recv[...].astype(F32)).astype(BF16)

    rs_copies = []
    for d in range(1, n):
        there = lax.rem(slab + d, n)
        copy = remote(
            total.at[:, pl.ds(pl.multiple_of(there * quarter, quarter), quarter)],
            rs_recv.at[d - 1],
            rs_send.at[d - 1],
            rs_recv_sem.at[d - 1],
            along(d),
        )
        copy.start()
        rs_copies.append(copy)
    mine = pl.ds(pl.multiple_of(slab * quarter, quarter), quarter)
    piece = total[:, mine, :].astype(F32)
    for d in range(1, n):
        rs_copies[d - 1].wait_recv()
        piece = piece + rs_recv[d - 1].astype(F32)
    piece = piece.astype(BF16)
    table[tile, core, mine, :] = piece[0]
    table[tile, core, nv:, :] = piece[1]

    ag_copies = []
    for d in range(1, n):
        own = table.at[tile, core, mine]
        copy = remote(own, own, ag_send.at[d - 1], ag_recv.at[d - 1], along(d))
        copy.start()
        ag_copies.append(copy)
    for copy in ag_copies:
        copy.wait_recv()
    bc_copies = []
    for i, (dt, dc) in enumerate(others):
        own = table.at[tile, core]
        copy = remote(own, own, bc_send.at[i], bc_recv.at[i], across(dt, dc))
        copy.start()
        bc_copies.append(copy)
    for copy in bc_copies:
        copy.wait_recv()

    def expander(count, width):
        row = lax.broadcasted_iota(jnp.int32, (count, width), 0)
        col = lax.broadcasted_iota(jnp.int32, (count, width), 1)
        inside = (row >= NS * col) & (row < NS * col + NS)
        return jnp.where(inside, 1.0, 0.0).astype(BF16)

    spread_rows = expander(NS * nv, nv)
    spread_cols = expander(cols, quarter)
    same = (
        lax.broadcasted_iota(jnp.int32, (NS * nv, cols), 0) & (NS - 1)
    ) == (lax.broadcasted_iota(jnp.int32, (NS * nv, cols), 1) & (NS - 1))

    def select(which, part, lo, hi):
        chosen = table[0, part, lo:hi, :].astype(F32)
        for t in range(1, tiles):
            here = jnp.full((hi - lo, nv), which, jnp.int32) == t
            chosen = jnp.where(here, table[t, part, lo:hi, :].astype(F32), chosen)
        return chosen.astype(BF16)

    @pl.loop(0, pair_count)
    def _(p):
        source = pairs_ref[p, 1]
        for part in range(2):
            narrow = select(source, part, nv, nv + quarter)
            wide = dot(spread_cols, narrow).astype(BF16)
            full = dot(spread_rows, wide, ((1,), (1,)))
            kbuf[p, part] = jnp.where(same, full, 0.0).astype(BF16)

    for d in range(n):
        k = lax.rem(slab + n - d, n)
        if d:
            p_copies[d - 1].wait_recv()
        block = pl.ds(pl.multiple_of(k * cols, cols), cols)

        @pl.loop(0, pair_count)
        def _(p):
            if d:
                p_real, p_imag = pg[d - 1, p, 0], pg[d - 1, p, 1]
            else:
                p_real, p_imag = p_ref[p, 0], p_ref[p, 1]
            k_real = kbuf[p, 0, block, :]
            k_imag = kbuf[p, 1, block, :]
            real = dot(p_real, k_real) - dot(p_imag, k_imag)
            imag = dot(p_real, k_imag) + dot(p_imag, k_real)
            if d:
                rbuf[p, 0] += real
                rbuf[p, 1] += imag
            else:
                rbuf[p, 0] = real
                rbuf[p, 1] = imag

    @pl.loop(0, pair_count)
    def _(p):
        sink = pairs_ref[p, 0]
        e_real = select(sink, 0, 0, nv)
        e_imag = select(sink, 1, 0, nv)
        for a in range(rows // nv):
            at = slice(a * nv, (a + 1) * nv)
            r_real = rbuf[p, 0, at, :].astype(BF16)
            r_imag = rbuf[p, 1, at, :].astype(BF16)
            out_ref[p, 0, at, :] = (dot(e_real, r_real) - dot(e_imag, r_imag)).astype(BF16)
            out_ref[p, 1, at, :] = (dot(e_real, r_imag) + dot(e_imag, r_real)).astype(BF16)

    for copy in p_copies + [core_copy] + rs_copies + ag_copies + bc_copies:
        copy.wait_send()


def link_weights(link_field, momenta, displacement, planes, sites, lattice_x):
    x_global = lax.axis_index("slab") * planes + jnp.arange(planes, dtype=jnp.int32)
    yz_global = lax.axis_index("spin") * sites + jnp.arange(sites, dtype=jnp.int32)
    forward = displacement == 1
    x_used = x_global[None, :] + jnp.where(forward, 0, 1)[:, None]
    cosine, minus_sine = phase_table(momenta, x_used, yz_global, lattice_x, LY, LZ)
    psi_imag = jnp.where(forward[:, None, None], -minus_sine, minus_sine)
    psi_real = cosine[:, None, None]
    psi_imag = psi_imag[:, None, None]
    u_real = jnp.swapaxes(link_field[0], 0, 1)[None]
    u_imag = -jnp.swapaxes(link_field[1], 0, 1)[None]
    w_real = psi_real * u_real - psi_imag * u_imag
    w_imag = psi_real * u_imag + psi_imag * u_real
    both = jnp.stack([w_real, w_imag], axis=3)
    flat = both.reshape(-1, planes, sites).transpose(1, 0, 2)
    return jnp.pad(flat, ((0, 0), (0, -flat.shape[1] % 8), (0, 0)))


def body(mesh, eigenvectors, gauge_links, momenta, displacement, slice_pairs, perambulators):
    n, tiles, cores = (mesh.shape[name] for name in ("slab", "tile", "spin"))
    field = eigenvectors[0]
    _, _, planes, sites, nv = field.shape
    pair_count, _, rows, cols = perambulators.shape
    lattice_x = planes * n
    normalize = 1.0 / math.sqrt(3072 * lattice_x * LY * LZ)
    weights = link_weights(gauge_links[0], momenta, displacement, planes, sites, lattice_x)
    quarter = nv // n
    dma = pltpu.SemaphoreType.DMA
    flops = 2 * (planes * 3 * sites * nv * nv * 8 + pair_count * 4 * rows * n * cols * cols)
    return pl.pallas_call(
        functools.partial(kernel, n, tiles, cores, normalize),
        out_shape=jax.ShapeDtypeStruct(perambulators.shape, BF16),
        in_specs=[pl.BlockSpec(memory_space=pltpu.VMEM)] * 3
        + [pl.BlockSpec(memory_space=pltpu.SMEM)] * 2,
        out_specs=pl.BlockSpec(memory_space=pltpu.VMEM),
        scratch_shapes=[
            pltpu.VMEM((2, 3, sites, nv), BF16),
            pltpu.VMEM((planes * 3, sites, 4 * nv), BF16),
            pltpu.VMEM((planes, sites, weights.shape[1]), F32),
            pltpu.VMEM((2, nv, 4 * nv), F32),
            pltpu.VMEM((2, 2, nv, nv), F32),
            pltpu.VMEM((2, nv, nv), BF16),
            pltpu.VMEM((2, nv, nv), BF16),
            pltpu.VMEM((2, nv, nv), BF16),
            pltpu.VMEM((n - 1, 2, quarter, nv), BF16),
            pltpu.VMEM((tiles, cores, nv + quarter, nv), BF16),
            pltpu.VMEM((n - 1,) + perambulators.shape, BF16),
            pltpu.VMEM((pair_count, 2, n * cols, cols), BF16),
            pltpu.VMEM((pair_count, 2, rows, cols), F32),
            dma((2,)),
            dma((n - 1,)),
            dma((n - 1,)),
            dma((2,)),
            dma((n - 1,)),
            dma((n - 1,)),
            dma((n - 1,)),
            dma((n - 1,)),
            dma((tiles * cores - 1,)),
            dma((tiles * cores - 1,)),
        ],
        compiler_params=pltpu.CompilerParams(
            collective_id=0, has_side_effects=True, vmem_limit_bytes=56 * 1024 * 1024
        ),
        cost_estimate=pl.CostEstimate(flops=flops, bytes_accessed=8 << 20, transcendentals=0),
    )(field, weights, perambulators, slice_pairs, displacement)


def solution(mesh):
    return jax.shard_map(
        functools.partial(body, mesh),
        mesh=mesh,
        in_specs=(
            P(("cfg", "tile"), None, None, "slab", "spin", None),
            P(("cfg", "tile"), None, None, None, "slab", "spin"),
            P(),
            P(),
            P("tile", None),
            P(("cfg", "tile"), None, "spin", "slab"),
        ),
        out_specs=P(("cfg", "tile"), None, "spin", "slab"),
        check_vma=False,
    )
```

time: 281 us -> 163 us (0.58)
  Pallas kernels: 0 us -> 155 us
  waiting for transfers between devices: 119 us -> 0 us
  blocking collectives: 60.3 us -> 0 us
  other arithmetic: 34.6 us -> 2.66 us
  local copies, waits for them, and re-layouts: 34.5 us -> 3.97 us
  between operations: 15.2 us -> 0.05 us
  matrix products: 12.3 us -> 0 us
  starting transfers between devices: 5.09 us -> 0 us
    pallas_call x0 -> x1, Pallas kernels: none -> 155 us  [body(): pl.pallas_call(functools.partial(kernel, n, tiles, cores, normalize), out...]
    all_gather x2 -> x0, waiting for transfers between devices: 99.5 us -> none  [the longest x1 79.2 us: body(): piece = lax.all_gather(left_split, 'slab', axis=3, tiled=True)]
    psum x1 -> x0, blocking collectives: 60.3 us -> none  [body(): summed = lax.psum(partial_sum, ('slab', 'spin'))]
    ppermute x1 -> x0, waiting for transfers between devices: 19 us -> none  [from_behind(): return lax.ppermute(x, axis, [(i, (i + by) % count) for i in range(count)])]
    slice x12 -> x1, local copies, waits for them, and re-layouts: 16.7 us -> 1 us  [phase_table(): wave_x = jnp.mod(momenta[:, 0:1] * x_global, extent_x)]
    dot_general x14 -> x0, matrix products: 12.3 us -> none  [the longest x2 3.58 us: complex_product(): jnp.einsum(form, first_imag, second_imag, preferred_element_type=jnp.floa...]
    select_n x4 -> x0, other arithmetic: 9.44 us -> none  [the longest x1 7.8 us: elemental_reindexed(): moved = jnp.where(is_forward, forward, backward_here)]
    convert_element_type x4 -> x0, other arithmetic: 8.34 us -> none  [the longest x2 5.05 us: color_apply(): field_real = vectors_here[0].astype(jnp.float32)]
  transfers between devices with their start and end apart: 3 -> 0, of which waited for: 3 -> 0; matrix products, arithmetic and copies ran while one was open for 6% -> 0% of each run, Pallas kernels for 0% -> 0%
where the time goes in v1:
time: 163 us; the launch traced here: 162 us
  Pallas kernels  155 us (95%)
  local copies, waits for them, and re-layouts  3.97 us (2%)
  other arithmetic  2.66 us (2%)
    pallas_call x1, Pallas kernels, body(): pl.pallas_call(functools.partial(kernel, n, tiles, cores, normalize), out...  155 us

profile of v1, /device:TPU:0, one launch (start us, length us, event | category | flops | bytes accessed | tf_op | source)
XLA Modules:
  0.0 161.5 jit_solution(11043228830191490848)
XLA Ops:
  0.0 0.7 broadcast_compare_fusion
  0.7 0.7 iota_add_fusion.1
  1.3 1.0 slice_reduce_fusion.2
  2.3 0.1 fusion.8
  2.4 0.1 fusion.3
  2.5 0.2 fusion
  2.7 0.8 slice_bitcast_fusion
  3.5 0.1 multiply_subtract_fusion
  3.6 0.1 pad_maximum_fusion
  3.7 0.7 pad.4.w_ref
  4.4 154.9 %shard_map.64 = bf16[2,2,512,256]{3,2,1,0:T(8,128)(2,1)} custom-call(bf16[2,3,2,512,256]{4,3,2,1,0:T(8,128)(2,1)} %bitcast.15, f32[2,40,512]{2,1,0:T(8,128)} %pad.4.w_ref, bf16[2,2,512,256]{3,2,1,0:T(8,128)(2,1)} %p_ref.1, s32[2,2]{1,0:T(2,128)} %pairs_ref.1, s32[2]{0:T(128)} %disp_ref.1), custom_call_target="tpu_custom_call" | custom-call | flops 5368709120 | bytes 8388608 | tf_op jit(solution)/shard_map/pallas_call | solution.py:287
  159.3 2.3 %copy.19 = bf16[2,2,512,256]{3,2,1,0:T(8,128)(2,1)} copy(bf16[2,2,512,256]{3,2,1,0:T(8,128)(2,1)} %shard_map.64) | data formatting | bytes 2097152
  (2 shorter events, 0.0 us)

commit v2 on v1

--- a/solution.py
+++ b/solution.py
@@ -49,8 +49,10 @@
 def kernel(
     n, tiles, cores, normalize,
     v_ref, w_ref, p_ref, pairs_ref, disp_ref, out_ref,
-    halo, ccat, wt, acc, parts, core_send, core_recv, total, rs_recv, table, pg, kbuf, rbuf,
-    halo_sem, p_send, p_recv, core_sem, rs_send, rs_recv_sem, ag_send, ag_recv, bc_send, bc_recv,
+    halo, ccat, wt, acc, parts, core_send, core_recv, total, rs_recv, table, pg, kbuf,
+    part_send, part_recv,
+    halo_sem, p_send, p_recv, core_sem, rs_send, rs_recv_sem, ag_send, ag_recv, x_send, x_recv,
+    share_sem, end_send, end_recv,
 ):
     slab = lax.axis_index("slab")
     tile = lax.axis_index("tile")
@@ -58,10 +60,21 @@
     _, _, planes, sites, nv = v_ref.shape
     pair_count, _, rows, cols = p_ref.shape
     quarter = nv // n
+    spins = rows // nv
+    chunks = [(p, a) for p in range(pair_count) for a in range(spins)]
+    line = n == 4
+    middle = (slab == 1) | (slab == 2)
+    end = jnp.where(slab == 1, 0, n - 1)
     others = [(dt, dc) for dt in range(tiles) for dc in range(cores) if (dt, dc) != (0, 0)]
 
     def along(d):
         return {"slab": lax.rem(slab + d, n)}
+
+    def gathers(who):
+        return (who == 1) | (who == 2)
+
+    def only(condition):
+        return pl.when(condition) if line else (lambda f: f())
 
     def across(dt, dc):
         return {"tile": lax.rem(tile + dt, tiles), "spin": lax.rem(core + dc, cores)}
@@ -117,11 +130,24 @@
                 )
 
     halo_copy.wait_send()
-    p_copies = []
-    for d in range(1, n):
-        copy = remote(p_ref, pg.at[d - 1], p_send.at[d - 1], p_recv.at[d - 1], along(d))
-        copy.start()
-        p_copies.append(copy)
+
+    def p_copy(i, d):
+        p, a = chunks[i]
+        return remote(
+            p_ref.at[p, :, a * nv : (a + 1) * nv],
+            pg.at[d - 1, p, :, a * nv : (a + 1) * nv],
+            p_send.at[d - 1, i],
+            p_recv.at[d - 1, i],
+            along(d),
+        )
+
+    for i in range(len(chunks)):
+        for d in range(1, n):
+
+            @only(gathers(lax.rem(slab + d, n)))
+            def _(i=i, d=d):
+                p_copy(i, d).start()
+
     halo_copy.wait_recv()
 
     @pl.loop(0, 3)
@@ -168,25 +194,32 @@
         rs_copies[d - 1].wait_recv()
         piece = piece + rs_recv[d - 1].astype(F32)
     piece = piece.astype(BF16)
-    table[tile, core, mine, :] = piece[0]
-    table[tile, core, nv:, :] = piece[1]
-
+    table[core, tile, 0, mine, :] = piece[0]
+    table[core, tile, 1, mine, :] = piece[1]
+
+    own = table.at[core, tile, :, mine]
     ag_copies = []
     for d in range(1, n):
-        own = table.at[tile, core, mine]
         copy = remote(own, own, ag_send.at[d - 1], ag_recv.at[d - 1], along(d))
         copy.start()
         ag_copies.append(copy)
-    for copy in ag_copies:
+    x_copies = []
+    for d in range(n):
+        if d:
+            ag_copies[d - 1].wait_recv()
+        k = lax.rem(slab + n - d, n)
+        held = table.at[core, tile, :, pl.ds(pl.multiple_of(k * quarter, quarter), quarter)]
+        for dt in range(1, tiles):
+            copy = remote(held, held, x_send.at[dt - 1, d], x_recv.at[dt - 1, d], across(dt, 0))
+            copy.start()
+            x_copies.append(copy)
+    for copy in x_copies:
         copy.wait_recv()
-    bc_copies = []
-    for i, (dt, dc) in enumerate(others):
-        own = table.at[tile, core]
-        copy = remote(own, own, bc_send.at[i], bc_recv.at[i], across(dt, dc))
-        copy.start()
-        bc_copies.append(copy)
-    for copy in bc_copies:
-        copy.wait_recv()
+    share = remote(
+        table.at[core], table.at[core], share_sem.at[0], share_sem.at[1], {"spin": 1 - core}
+    )
+    share.start()
+    share.wait_recv()
 
     def expander(count, width):
         row = lax.broadcasted_iota(jnp.int32, (count, width), 0)
@@ -200,58 +233,108 @@
         lax.broadcasted_iota(jnp.int32, (NS * nv, cols), 0) & (NS - 1)
     ) == (lax.broadcasted_iota(jnp.int32, (NS * nv, cols), 1) & (NS - 1))
 
-    def select(which, part, lo, hi):
-        chosen = table[0, part, lo:hi, :].astype(F32)
+    def select(which, part, elemental, at, count):
+        chosen = table[part, 0, elemental, at, :].astype(F32)
         for t in range(1, tiles):
-            here = jnp.full((hi - lo, nv), which, jnp.int32) == t
-            chosen = jnp.where(here, table[t, part, lo:hi, :].astype(F32), chosen)
+            here = jnp.full((count, nv), which, jnp.int32) == t
+            chosen = jnp.where(here, table[part, t, elemental, at, :].astype(F32), chosen)
         return chosen.astype(BF16)
 
-    @pl.loop(0, pair_count)
-    def _(p):
-        source = pairs_ref[p, 1]
-        for part in range(2):
-            narrow = select(source, part, nv, nv + quarter)
-            wide = dot(spread_cols, narrow).astype(BF16)
-            full = dot(spread_rows, wide, ((1,), (1,)))
-            kbuf[p, part] = jnp.where(same, full, 0.0).astype(BF16)
-
-    for d in range(n):
-        k = lax.rem(slab + n - d, n)
-        if d:
-            p_copies[d - 1].wait_recv()
-        block = pl.ds(pl.multiple_of(k * cols, cols), cols)
+    def widen(side, owner):
+        at = pl.ds(pl.multiple_of(owner * quarter, quarter), quarter)
 
         @pl.loop(0, pair_count)
         def _(p):
-            if d:
-                p_real, p_imag = pg[d - 1, p, 0], pg[d - 1, p, 1]
-            else:
-                p_real, p_imag = p_ref[p, 0], p_ref[p, 1]
-            k_real = kbuf[p, 0, block, :]
-            k_imag = kbuf[p, 1, block, :]
-            real = dot(p_real, k_real) - dot(p_imag, k_imag)
-            imag = dot(p_real, k_imag) + dot(p_imag, k_real)
-            if d:
-                rbuf[p, 0] += real
-                rbuf[p, 1] += imag
-            else:
-                rbuf[p, 0] = real
-                rbuf[p, 1] = imag
-
-    @pl.loop(0, pair_count)
-    def _(p):
-        sink = pairs_ref[p, 0]
-        e_real = select(sink, 0, 0, nv)
-        e_imag = select(sink, 1, 0, nv)
-        for a in range(rows // nv):
-            at = slice(a * nv, (a + 1) * nv)
-            r_real = rbuf[p, 0, at, :].astype(BF16)
-            r_imag = rbuf[p, 1, at, :].astype(BF16)
-            out_ref[p, 0, at, :] = (dot(e_real, r_real) - dot(e_imag, r_imag)).astype(BF16)
-            out_ref[p, 1, at, :] = (dot(e_real, r_imag) + dot(e_imag, r_real)).astype(BF16)
-
-    for copy in p_copies + [core_copy] + rs_copies + ag_copies + bc_copies:
+            for part in range(2):
+                narrow = select(pairs_ref[p, 1], part, 1, at, quarter)
+                wide = dot(spread_cols, narrow).astype(BF16)
+                full = dot(spread_rows, wide, ((1,), (1,)))
+                kbuf[side, p, part] = jnp.where(same, full, 0.0).astype(BF16)
+
+    def term(i, d, side):
+        p, a = chunks[i]
+        at = slice(a * nv, (a + 1) * nv)
+        k = lax.rem(slab + n - d, n)
+        block = pl.ds(pl.multiple_of(k * cols, cols), cols)
+        if d:
+            p_real, p_imag = pg[d - 1, p, 0, at, :], pg[d - 1, p, 1, at, :]
+        else:
+            p_real, p_imag = p_ref[p, 0, at, :], p_ref[p, 1, at, :]
+        k_real = kbuf[side, p, 0, block, :]
+        k_imag = kbuf[side, p, 1, block, :]
+        real = dot(p_real, k_real) - dot(p_imag, k_imag)
+        imag = dot(p_real, k_imag) + dot(p_imag, k_real)
+        return real, imag
+
+    def add(x, y):
+        return x[0] + y[0], x[1] + y[1]
+
+    def finish(i, right):
+        p, a = chunks[i]
+        at = slice(a * nv, (a + 1) * nv)
+        e_real = select(pairs_ref[p, 0], 0, 0, slice(0, nv), nv)
+        e_imag = select(pairs_ref[p, 0], 1, 0, slice(0, nv), nv)
+        r_real = right[0].astype(BF16)
+        r_imag = right[1].astype(BF16)
+        out_ref[p, 0, at, :] = (dot(e_real, r_real) - dot(e_imag, r_imag)).astype(BF16)
+        out_ref[p, 1, at, :] = (dot(e_real, r_imag) + dot(e_imag, r_real)).astype(BF16)
+
+    def end_copy(i):
+        return remote(
+            part_send.at[i], part_recv.at[i], end_send.at[i], end_recv.at[i], {"slab": end}
+        )
+
+    @only(middle)
+    def _():
+        if line:
+            widen(1, end)
+        else:
+            widen(0, slab)
+        for i in range(len(chunks)):
+            for d in range(1, n):
+                p_copy(i, d).wait_recv()
+            if line:
+                toward = term(i, 0, 1)
+                toward = add(toward, term(i, 2, 1))
+                first = jnp.full((nv, cols), slab, jnp.int32) == 1
+                low = term(i, 1, 1)
+                high = term(i, n - 1, 1)
+                toward = (
+                    toward[0] + jnp.where(first, high[0], low[0]),
+                    toward[1] + jnp.where(first, high[1], low[1]),
+                )
+                part_send[i, 0] = toward[0].astype(BF16)
+                part_send[i, 1] = toward[1].astype(BF16)
+                end_copy(i).start()
+                if i == 0:
+                    widen(0, slab)
+            right = term(i, 0, 0)
+            for d in range(1, n):
+                right = add(right, term(i, d, 0))
+            finish(i, right)
+        if line:
+            for i in range(len(chunks)):
+                end_copy(i).wait_send()
+
+    if line:
+
+        @pl.when(jnp.logical_not(middle))
+        def _():
+            widen(0, slab)
+            for i in range(len(chunks)):
+                right = term(i, 0, 0)
+                end_copy(i).wait_recv()
+                rest = (part_recv[i, 0].astype(F32), part_recv[i, 1].astype(F32))
+                finish(i, add(right, rest))
+
+    for i in range(len(chunks)):
+        for d in range(1, n):
+
+            @only(gathers(lax.rem(slab + d, n)))
+            def _(i=i, d=d):
+                p_copy(i, d).wait_send()
+
+    for copy in [core_copy, share] + rs_copies + ag_copies + x_copies:
         copy.wait_send()
 
 
@@ -282,6 +365,7 @@
     normalize = 1.0 / math.sqrt(3072 * lattice_x * LY * LZ)
     weights = link_weights(gauge_links[0], momenta, displacement, planes, sites, lattice_x)
     quarter = nv // n
+    chunks = pair_count * (rows // nv)
     dma = pltpu.SemaphoreType.DMA
     flops = 2 * (planes * 3 * sites * nv * nv * 8 + pair_count * 4 * rows * n * cols * cols)
     return pl.pallas_call(
@@ -300,20 +384,24 @@
             pltpu.VMEM((2, nv, nv), BF16),
             pltpu.VMEM((2, nv, nv), BF16),
             pltpu.VMEM((n - 1, 2, quarter, nv), BF16),
-            pltpu.VMEM((tiles, cores, nv + quarter, nv), BF16),
+            pltpu.VMEM((cores, tiles, 2, nv, nv), BF16),
             pltpu.VMEM((n - 1,) + perambulators.shape, BF16),
-            pltpu.VMEM((pair_count, 2, n * cols, cols), BF16),
-            pltpu.VMEM((pair_count, 2, rows, cols), F32),
+            pltpu.VMEM((2, pair_count, 2, n * cols, cols), BF16),
+            pltpu.VMEM((chunks, 2, nv, cols), BF16),
+            pltpu.VMEM((chunks, 2, nv, cols), BF16),
             dma((2,)),
-            dma((n - 1,)),
-            dma((n - 1,)),
+            dma((n - 1, chunks)),
+            dma((n - 1, chunks)),
             dma((2,)),
             dma((n - 1,)),
             dma((n - 1,)),
             dma((n - 1,)),
             dma((n - 1,)),
-            dma((tiles * cores - 1,)),
-            dma((tiles * cores - 1,)),
+            dma((tiles - 1, n)),
+            dma((tiles - 1, n)),
+            dma((2,)),
+            dma((chunks,)),
+            dma((chunks,)),
         ],
         compiler_params=pltpu.CompilerParams(
             collective_id=0, has_side_effects=True, vmem_limit_bytes=56 * 1024 * 1024

time: 163 us -> 140 us (0.86)
  Pallas kernels: 155 us -> 133 us
    pallas_call x1, Pallas kernels: 155 us -> 133 us  [body(): pl.pallas_call(functools.partial(kernel, n, tiles, cores, normalize), out...]
where the time goes in v2:
time: 140 us; the launch traced here: 139 us
  Pallas kernels  133 us (95%)
  local copies, waits for them, and re-layouts  3.97 us (3%)
  other arithmetic  2.66 us (2%)
    pallas_call x1, Pallas kernels, body(): pl.pallas_call(functools.partial(kernel, n, tiles, cores, normalize), out...  133 us

profile of v2, /device:TPU:0, one launch (start us, length us, event | category | flops | bytes accessed | tf_op | source)
XLA Modules:
  0.0 139.4 jit_solution(1736657153182575099)
XLA Ops:
  0.0 0.7 broadcast_compare_fusion
  0.7 0.7 iota_add_fusion.1
  1.3 1.0 slice_reduce_fusion.2
  2.3 0.1 fusion.8
  2.4 0.1 fusion.3
  2.5 0.2 fusion
  2.7 0.8 slice_bitcast_fusion
  3.5 0.1 multiply_subtract_fusion
  3.6 0.1 pad_maximum_fusion
  3.7 0.7 pad.4.w_ref
  4.4 132.7 %shard_map.64 = bf16[2,2,512,256]{3,2,1,0:T(8,128)(2,1)} custom-call(bf16[2,3,2,512,256]{4,3,2,1,0:T(8,128)(2,1)} %bitcast.15, f32[2,40,512]{2,1,0:T(8,128)} %pad.4.w_ref, bf16[2,2,512,256]{3,2,1,0:T(8,128)(2,1)} %p_ref.1, s32[2,2]{1,0:T(2,128)} %pairs_ref.1, s32[2]{0:T(128)} %disp_ref.1), custom_call_target="tpu_custom_call" | custom-call | flops 5368709120 | bytes 8388608 | tf_op jit(solution)/shard_map/pallas_call | solution.py:371
  137.1 2.3 %copy.19 = bf16[2,2,512,256]{3,2,1,0:T(8,128)(2,1)} copy(bf16[2,2,512,256]{3,2,1,0:T(8,128)(2,1)} %shard_map.64) | data formatting | bytes 2097152
  (2 shorter events, 0.0 us)

commit v3 on v2

--- a/solution.py
+++ b/solution.py
@@ -86,10 +86,13 @@
         pl.semaphore_signal(barrier, inc=1, device_id=across(dt, dc), device_id_type=MESH)
     pl.semaphore_wait(barrier, n - 1 + len(others))
 
-    halo_copy = remote(
-        v_ref.at[:, :, 0], halo, halo_sem.at[0], halo_sem.at[1], along(n - 1)
-    )
-    halo_copy.start()
+    halo_copies = []
+    for c in range(3):
+        copy = remote(
+            v_ref.at[:, c, 0], halo.at[:, c], halo_sem.at[0, c], halo_sem.at[1, c], along(n - 1)
+        )
+        copy.start()
+        halo_copies.append(copy)
 
     for plane in range(planes):
         wt[plane] = w_ref[plane].T
@@ -129,7 +132,8 @@
                     v_ref[part, c, plane + 1], ccat[plane * 3 + c], ((0,), (0,))
                 )
 
-    halo_copy.wait_send()
+    for copy in halo_copies:
+        copy.wait_send()
 
     def p_copy(i, d):
         p, a = chunks[i]
@@ -141,17 +145,18 @@
             along(d),
         )
 
-    for i in range(len(chunks)):
-        for d in range(1, n):
-
-            @only(gathers(lax.rem(slab + d, n)))
-            def _(i=i, d=d):
-                p_copy(i, d).start()
-
-    halo_copy.wait_recv()
-
-    @pl.loop(0, 3)
-    def _(c):
+    def p_start(which):
+        for i in which:
+            for d in range(1, n):
+
+                @only(gathers(lax.rem(slab + d, n)))
+                def _(i=i, d=d):
+                    p_copy(i, d).start()
+
+    p_start(range(1))
+
+    for c in range(3):
+        halo_copies[c].wait_recv()
         for part in range(2):
             acc[part] += dot(halo[part, c], ccat[(planes - 1) * 3 + c], ((0,), (0,)))
 
@@ -203,6 +208,7 @@
         copy = remote(own, own, ag_send.at[d - 1], ag_recv.at[d - 1], along(d))
         copy.start()
         ag_copies.append(copy)
+    p_start(range(1, 2))
     x_copies = []
     for d in range(n):
         if d:
@@ -213,6 +219,7 @@
             copy = remote(held, held, x_send.at[dt - 1, d], x_recv.at[dt - 1, d], across(dt, 0))
             copy.start()
             x_copies.append(copy)
+    p_start(range(2, len(chunks)))
     for copy in x_copies:
         copy.wait_recv()
     share = remote(
@@ -256,7 +263,7 @@
         at = slice(a * nv, (a + 1) * nv)
         k = lax.rem(slab + n - d, n)
         block = pl.ds(pl.multiple_of(k * cols, cols), cols)
-        if d:
+        if not isinstance(d, int) or d:
             p_real, p_imag = pg[d - 1, p, 0, at, :], pg[d - 1, p, 1, at, :]
         else:
             p_real, p_imag = p_ref[p, 0, at, :], p_ref[p, 1, at, :]
@@ -296,13 +303,7 @@
             if line:
                 toward = term(i, 0, 1)
                 toward = add(toward, term(i, 2, 1))
-                first = jnp.full((nv, cols), slab, jnp.int32) == 1
-                low = term(i, 1, 1)
-                high = term(i, n - 1, 1)
-                toward = (
-                    toward[0] + jnp.where(first, high[0], low[0]),
-                    toward[1] + jnp.where(first, high[1], low[1]),
-                )
+                toward = add(toward, term(i, jnp.where(slab == 1, n - 1, 1), 1))
                 part_send[i, 0] = toward[0].astype(BF16)
                 part_send[i, 1] = toward[1].astype(BF16)
                 end_copy(i).start()
@@ -389,7 +390,7 @@
             pltpu.VMEM((2, pair_count, 2, n * cols, cols), BF16),
             pltpu.VMEM((chunks, 2, nv, cols), BF16),
             pltpu.VMEM((chunks, 2, nv, cols), BF16),
-            dma((2,)),
+            dma((2, 3)),
             dma((n - 1, chunks)),
             dma((n - 1, chunks)),
             dma((2,)),

time: 140 us -> 114 us (0.81)
  Pallas kernels: 133 us -> 106 us
    pallas_call x1, Pallas kernels: 133 us -> 106 us  [body(): pl.pallas_call(functools.partial(kernel, n, tiles, cores, normalize), out...]
where the time goes in v3:
time: 114 us; the launch traced here: 113 us
  Pallas kernels  106 us (93%)
  local copies, waits for them, and re-layouts  3.97 us (3%)
  other arithmetic  2.66 us (2%)
    pallas_call x1, Pallas kernels, body(): pl.pallas_call(functools.partial(kernel, n, tiles, cores, normalize), out...  106 us

profile of v3, /device:TPU:0, one launch (start us, length us, event | category | flops | bytes accessed | tf_op | source)
XLA Modules:
  0.0 113.0 jit_solution(9439501703299855427)
XLA Ops:
  0.0 0.7 broadcast_compare_fusion
  0.7 0.7 iota_add_fusion.1
  1.3 1.0 slice_reduce_fusion.2
  2.3 0.1 fusion.8
  2.4 0.1 fusion.3
  2.5 0.2 fusion
  2.7 0.8 slice_bitcast_fusion
  3.5 0.1 multiply_subtract_fusion
  3.6 0.1 pad_maximum_fusion
  3.7 0.7 pad.4.w_ref
  4.4 106.3 %shard_map.64 = bf16[2,2,512,256]{3,2,1,0:T(8,128)(2,1)} custom-call(bf16[2,3,2,512,256]{4,3,2,1,0:T(8,128)(2,1)} %bitcast.15, f32[2,40,512]{2,1,0:T(8,128)} %pad.4.w_ref, bf16[2,2,512,256]{3,2,1,0:T(8,128)(2,1)} %p_ref.1, s32[2,2]{1,0:T(2,128)} %pairs_ref.1, s32[2]{0:T(128)} %disp_ref.1), custom_call_target="tpu_custom_call" | custom-call | flops 5368709120 | bytes 8388608 | tf_op jit(solution)/shard_map/pallas_call | solution.py:372
  110.8 2.3 %copy.19 = bf16[2,2,512,256]{3,2,1,0:T(8,128)(2,1)} copy(bf16[2,2,512,256]{3,2,1,0:T(8,128)(2,1)} %shard_map.64) | data formatting | bytes 2097152
  (2 shorter events, 0.0 us)
